TPU v7x, 128 devices: a whole 4x4x4 slice. The times are simulated.
128 devices in a mesh: gx: 8 (over z, core), gy: 16 (over x, y).
Axes of the slice: x: 4, y: 4, z: 4, core: 2. Of those that a mesh axis runs over, the one named last changes fastest.
Arguments:
- tokens: bfloat16 [200704, 1024], P(('gx', 'gy')), may hold values from -6 to 6
- image_slot: int32 [1024], replicated, may hold values from 0 to 1023, as said below
- pairs: int32 [1024, 2], P(('gx', 'gy')), may hold values from 0 to 1023, as said below
- w_embed: bfloat16 [1024, 768], replicated, may hold values from -0.1875 to 0.1875
- gain_query: float32 [768], replicated, may hold values from 0.1 to 1.9
- gain_key: float32 [768], replicated, may hold values from 0.1 to 1.9
- w_query: bfloat16 [768, 768], replicated, may hold values from -0.21875 to 0.21875
- w_key: bfloat16 [768, 768], replicated, may hold values from -0.21875 to 0.21875
- w_value: bfloat16 [768, 768], replicated, may hold values from -0.21875 to 0.21875
- w_out: bfloat16 [768, 768], replicated, may hold values from -0.21875 to 0.21875
- gain_head: float32 [768], replicated, may hold values from 0.1 to 1.9
- w_head: bfloat16 [768, 1024], replicated, may hold values from -0.21875 to 0.21875
Outputs:
- point_sums: float32 [200704, 1024], P(('gx', 'gy'))
Inputs may be any that keep to these rules, and one draw needn't show every extreme that they name: `image_slot`: A permutation: each slot holds one image. Device w = a * 16 + b (gx index a, gy index b) holds pairs w * 8 to (w + 1) * 8 - 1. The device owning slot s is s // 8. For every pair of device (a, b), its first image's owner has gx index a and its second image's owner has gy index b. The first images of one device's pairs have owners of different gy indices (1 at most per owner); the second images have at most 2 owners alike in gx index, exactly 2 for some. The two images of a pair differ.
All inputs are finite; a program needn't handle non-finite values.
Results may differ from a plain program's by a relative error of at most 0.011.
Values may be sent and summed in bfloat16 or wider, within the bound.
A program may use at most 256 MiB of HBM per device.

v0:
```python
import jax
import jax.numpy as jnp
from jax import lax
from jax.sharding import PartitionSpec as P

D_MODEL = 768
HEADS = 12
PATCHES = 196
PIXELS = 256
HEAD_OUT = 1024
CAP_FIRST = 1
CAP_SECOND = 2


def layer_norm(values, gain):
    mean = jnp.mean(values, axis=-1, keepdims=True)
    centered = values - mean
    spread = jnp.mean(centered * centered, axis=-1, keepdims=True)
    return centered * lax.rsqrt(spread + 1e-06) * gain


def cross_block(queries, keys, gain_query, gain_key, w_query, w_key, w_value, w_out):
    batch, patches, width = queries.shape
    head_dim = width // HEADS
    normed_q = (
        layer_norm(queries.astype(jnp.float32), gain_query)
        .astype(jnp.bfloat16)
        .reshape(batch * patches, width)
    )
    normed_k = (
        layer_norm(keys.astype(jnp.float32), gain_key)
        .astype(jnp.bfloat16)
        .reshape(batch * patches, width)
    )
    query_proj = jnp.dot(normed_q, w_query, preferred_element_type=jnp.float32).astype(jnp.bfloat16)
    key_proj = jnp.dot(normed_k, w_key, preferred_element_type=jnp.float32).astype(jnp.bfloat16)
    value_proj = jnp.dot(normed_k, w_value, preferred_element_type=jnp.float32).astype(jnp.bfloat16)
    query_proj = query_proj.reshape(batch, patches, HEADS, head_dim)
    key_proj = key_proj.reshape(batch, patches, HEADS, head_dim)
    value_proj = value_proj.reshape(batch, patches, HEADS, head_dim)
    scores = jnp.einsum(
        "bqhd,bkhd->bhqk", query_proj, key_proj, preferred_element_type=jnp.float32
    ) * head_dim ** (-0.5)
    expd = jnp.exp(scores)
    weights = (expd / jnp.sum(expd, axis=-1, keepdims=True)).astype(jnp.bfloat16)
    attended = jnp.einsum(
        "bhqk,bkhd->bqhd", weights, value_proj, preferred_element_type=jnp.float32
    ).astype(jnp.bfloat16)
    mixed = jnp.dot(
        attended.reshape(batch * patches, width), w_out, preferred_element_type=jnp.float32
    )
    resid = queries.astype(jnp.float32).reshape(batch * patches, width) + mixed
    return resid.astype(jnp.bfloat16).reshape(batch, patches, width)


def point_head(resid, gain_head, w_head):
    batch, patches, width = resid.shape
    normed = (
        layer_norm(resid.astype(jnp.float32), gain_head)
        .astype(jnp.bfloat16)
        .reshape(batch * patches, width)
    )
    raw = jnp.dot(normed, w_head, preferred_element_type=jnp.float32)
    confidence = 1.0 + jnp.exp(raw[:, 3 * PIXELS :])
    weighted = raw[:, : 3 * PIXELS] * jnp.tile(confidence, (1, 3))
    joined = jnp.concatenate([weighted, confidence], axis=1).astype(jnp.bfloat16)
    return joined.reshape(batch, patches * 4 * PIXELS)


def locate(slots, images_here, columns):
    device = slots // images_here
    return (device // columns, device % columns, slots % images_here)


def ranks(target):
    count = target.shape[-1]
    same = target[..., :, None] == target[..., None, :]
    earlier = jnp.arange(count)[None, :] < jnp.arange(count)[:, None]
    return jnp.sum(same & earlier, axis=-1)


def owner_table(dest, mine, local, capacity, images_here):
    rank = ranks(dest)
    hits = (dest == mine)[..., None, None]
    hits = hits & (rank[..., None, None] == jnp.arange(capacity)[:, None])
    hits = hits & (local[..., None, None] == jnp.arange(images_here)[None, :])
    table = jnp.sum(hits.astype(jnp.int32), axis=1)
    return table.reshape(dest.shape[0] * capacity, images_here).astype(jnp.bfloat16)


def worker_table(dest, peers, capacity):
    rank = ranks(dest)
    hits = dest[:, None, None] == jnp.arange(peers)[None, :, None]
    hits = hits & (rank[:, None, None] == jnp.arange(capacity)[None, None, :])
    return hits.reshape(dest.shape[0], peers * capacity).astype(jnp.bfloat16)


def per_device(
    tokens,
    image_slot,
    pairs,
    w_embed,
    gain_query,
    gain_key,
    w_query,
    w_key,
    w_value,
    w_out,
    gain_head,
    w_head,
):
    row_count = lax.axis_size("gx")
    columns = lax.axis_size("gy")
    my_row = lax.axis_index("gx")
    my_col = lax.axis_index("gy")
    images_here = tokens.shape[0] // PATCHES
    count = pairs.shape[0]
    catalog = jnp.arange(image_slot.shape[0], dtype=jnp.int32)
    slots = jnp.sum(jnp.where(pairs[:, :, None] == catalog, image_slot, 0), axis=-1)
    every = lax.all_gather(slots, ("gx", "gy"), axis=0, tiled=True).reshape(
        row_count, columns, count, 2
    )
    unused_a, first_col, unused_b = locate(slots[:, 0], images_here, columns)
    second_row, unused_c, unused_d = locate(slots[:, 1], images_here, columns)
    pick_first = worker_table(first_col, columns, CAP_FIRST)
    pick_second = worker_table(second_row, row_count, CAP_SECOND)
    row_lists = lax.dynamic_index_in_dim(every, my_row, 0, keepdims=False)[:, :, 0]
    unused_e, dest_col, local_first = locate(row_lists, images_here, columns)
    table_first = owner_table(dest_col, my_col, local_first, CAP_FIRST, images_here)
    col_lists = lax.dynamic_index_in_dim(every, my_col, 1, keepdims=False)[:, :, 1]
    dest_row, unused_f, local_second = locate(col_lists, images_here, columns)
    table_second = owner_table(dest_row, my_row, local_second, CAP_SECOND, images_here)
    source = tokens.reshape(images_here, -1)
    send_first = jnp.dot(table_first, source, preferred_element_type=jnp.float32).astype(
        jnp.bfloat16
    )
    send_second = jnp.dot(table_second, source, preferred_element_type=jnp.float32).astype(
        jnp.bfloat16
    )
    got_first = lax.all_to_all(send_first, "gy", split_axis=0, concat_axis=0, tiled=True)
    got_second = lax.all_to_all(send_second, "gx", split_axis=0, concat_axis=0, tiled=True)
    view_first = jnp.dot(pick_first, got_first, preferred_element_type=jnp.float32).astype(
        jnp.bfloat16
    )
    view_second = jnp.dot(pick_second, got_second, preferred_element_type=jnp.float32).astype(
        jnp.bfloat16
    )
    views = jnp.concatenate([view_first, view_second], axis=0)
    views = jnp.dot(
        views.reshape(2 * count * PATCHES, -1), w_embed, preferred_element_type=jnp.float32
    )
    views = views.astype(jnp.bfloat16).reshape(2 * count, PATCHES, D_MODEL)
    keys = jnp.concatenate([views[count:], views[:count]], axis=0)
    resid = cross_block(views, keys, gain_query, gain_key, w_query, w_key, w_value, w_out)
    payload = point_head(resid, gain_head, w_head)
    back_first = jnp.dot(pick_first.T, payload[:count], preferred_element_type=jnp.float32).astype(
        jnp.bfloat16
    )
    back_second = jnp.dot(
        pick_second.T, payload[count:], preferred_element_type=jnp.float32
    ).astype(jnp.bfloat16)
    came_first = lax.all_to_all(back_first, "gy", split_axis=0, concat_axis=0, tiled=True)
    came_second = lax.all_to_all(back_second, "gx", split_axis=0, concat_axis=0, tiled=True)
    total = jnp.dot(table_first.T, came_first, preferred_element_type=jnp.float32)
    total = total + jnp.dot(table_second.T, came_second, preferred_element_type=jnp.float32)
    return total.reshape(images_here * PATCHES, HEAD_OUT)


def solution(mesh):
    return jax.shard_map(
        per_device,
        mesh=mesh,
        in_specs=(
            P(("gx", "gy"), None),
            P(),
            P(("gx", "gy"), None),
            P(),
            P(),
            P(),
            P(),
            P(),
            P(),
            P(),
            P(),
            P(),
        ),
        out_specs=P(("gx", "gy"), None),
        check_vma=False,
    )
```

profile of v0, /device:TPU:20, one launch (start us, length us, event | category | flops | bytes accessed | tf_op | source)
XLA Modules:
  0.0 811.3 jit_solution(437198485305227285)
XLA Ops:
  0.0 1.0 select_reduce_fusion
  1.0 54.3 %all-gather = s32[128,8,2]{1,2,0:T(2,128)S(1)} all-gather(s32[1,8,2]{1,2,0:T(2,128)S(1)} %bitcast.137), channel_id=1, replica_groups=mesh['gx'=8,'gy'=16] {'gx','gy'}, dimensions={0}, use_global_device_ids=true | all-gather | bytes 8256 | tf_op jit(solution)/shard_map/all_gather | solution.py:120
  55.9 7.7 reshape.669
  63.6 6.5 convolution_convert_fusion.2
  70.1 7.5 all_to_all.31
  77.6 4.9 all-to-all-start.1
  82.9 0.6 copy-done.8
  83.4 5.2 fusion
  89.2 16.9 %reduce.5 = bf16[16,200704]{1,0:T(8,128)(2,1)} reduce(bf16[16,1,200704]{2,0,1:T(8,128)(2,1)} %fusion, bf16[]{:T(256)} %broadcast.795), dimensions={1}, to_apply=%copy.95.reduce_sub_computation | reduce | bytes 12845058 | tf_op jit(solution)/shard_map/all_to_all | solution.py:140
  106.1 9.4 %reshape.685 = bf16[16,2,100352]{2,1,0:T(2,128)(2,1)} reshape(bf16[16,200704]{1,0:T(8,128)(2,1)} %reduce.5) | data formatting | bytes 12845056
  115.5 40.6 %all-to-all-done.1 = bf16[8,2,200704]{2,1,0:T(2,128)(2,1)} async-done(((bf16[8,2,200704]{2,1,0:T(2,128)(2,1)}), bf16[8,2,200704]{2,1,0:T(2,128)(2,1)}, u32[]{:S(2)}, u32[]{:S(2)}) %all-to-all-start.1) | async-done | bytes 6422560 | tf_op jit(solution)/shard_map/all_to_all | solution.py:141
  156.1 8.4 %all-to-all-start = ((bf16[16,2,100352]{2,1,0:T(2,128)(2,1)}), bf16[16,2,100352]{2,1,0:T(2,128)(2,1)}, u32[]{:S(2)}, u32[]{:S(2)}) async-start(bf16[16,2,100352]{2,1,0:T(2,128)(2,1)} %reshape.685), calls=%async_computation | async-start | bytes 12845056 | tf_op jit(solution)/shard_map/all_to_all | solution.py:140
  165.0 0.6 copy-done.10
  165.6 6.7 fusion.3
  172.3 90.8 %all-to-all-done = bf16[16,2,100352]{2,1,0:T(2,128)(2,1)} async-done(((bf16[16,2,100352]{2,1,0:T(2,128)(2,1)}), bf16[16,2,100352]{2,1,0:T(2,128)(2,1)}, u32[]{:S(2)}, u32[]{:S(2)}) %all-to-all-start) | async-done | bytes 6422560 | tf_op jit(solution)/shard_map/all_to_all | solution.py:140
  263.1 14.5 %reshape.686 = bf16[16,1,200704]{2,1,0:T(2,128)(2,1)} reshape(bf16[16,2,100352]{2,1,0:T(2,128)(2,1)} %all-to-all-done) | data formatting | bytes 12845056
  277.6 11.8 %convolution_convert_fusion.4 = bf16[8,200704]{1,0:T(8,128)(2,1)S(1)} fusion(bf16[16,1,200704]{2,1,0:T(2,128)(2,1)} %reshape.686, s32[8]{0:T(128)S(1)} %get-tuple-element.18, pred[8]{0:T(512)(128)(4,1)S(1)} %broadcast_compare_fusion.1), kind=kOutput, calls=%fused_computation.10 | convolution fusion | flops 52986112 | bytes 9633832 | tf_op jit(solution)/shard_map/dot_general | solution.py:142
  289.4 3.0 pad_maximum_fusion
  292.4 13.6 %reshape.670 = bf16[3136,1024]{1,0:T(8,128)(2,1)} reshape(bf16[16,200704]{1,0:T(8,128)(2,1)} %pad_maximum_fusion) | data formatting | bytes 12845056 | tf_op jit(solution)/shard_map/reshape | solution.py:150
  306.0 8.6 %convert_reduce_fusion = (f32[3136]{0:T(1024)S(1)}, bf16[3136,768]{1,0:T(8,128)(2,1)S(1)}) fusion(bf16[3136,1024]{1,0:T(8,128)(2,1)} %reshape.670, bf16[1024,768]{1,0:T(8,128)(2,1)S(1)} %copy-done.16), kind=kOutput, calls=%fused_computation.17 | convolution fusion | flops 4939723776 | bytes 12824832 | tf_op jit(solution)/shard_map/dot_general | solution.py:149
  314.7 2.3 copy-done.3
  317.0 2.5 fusion.79
  319.5 4.1 slice.49
  323.5 4.1 slice.47
  327.6 7.0 maximum_convert_fusion
  334.6 0.8 fusion.42
  335.4 3.1 multiply_reduce_fusion
  338.7 10.0 %reshape.676 = f32[3136,768]{1,0:T(8,128)} reshape(f32[16,196,768]{2,1,0:T(8,128)} %maximum_convert_fusion) | data formatting | bytes 19267584 | tf_op jit(solution)/shard_map/convert_element_type | solution.py:31
  348.8 9.0 %convolution_convert_fusion.5 = bf16[3136,768]{1,0:T(8,128)(2,1)} fusion(bf16[768,768]{1,0:T(8,128)(2,1)S(1)} %copy-done.17, f32[3136,768]{1,0:T(8,128)} %reshape.676, f32[768]{0:T(1024)S(1)} %copy-done.22, f32[3136]{0:T(1024)S(1)} %rsqrt.28, f32[3136]{0:T(1024)S(1)} %div.185), kind=kOutput, calls=%fused_computation.39 | convolution fusion | flops 3711418368 | bytes 15658496 | tf_op jit(solution)/shard_map/dot_general | solution.py:36
  357.7 15.4 %reshape.684 = bf16[16,196,12,64]{3,2,1,0:T(8,128)(2,1)} reshape(bf16[3136,768]{1,0:T(8,128)(2,1)} %convolution_convert_fusion.5) | data formatting | bytes 9633792 | tf_op jit(solution)/shard_map/reshape | solution.py:39
  373.1 3.9 fusion.14
  377.0 8.1 convolution_convert_fusion.6
  385.1 15.4 %reshape.683 = bf16[16,196,12,64]{3,2,1,0:T(8,128)(2,1)} reshape(bf16[3136,768]{1,0:T(8,128)(2,1)} %convolution_convert_fusion.6) | data formatting | bytes 9633792 | tf_op jit(solution)/shard_map/reshape | solution.py:38
  400.6 8.8 %convolution_convert_fusion.7 = bf16[3136,768]{1,0:T(8,128)(2,1)} fusion(bf16[768,768]{1,0:T(8,128)(2,1)S(1)} %copy-done.19, f32[3136,768]{1,0:T(8,128)} %reshape.676, f32[768]{0:T(1024)S(1)} %copy-done.22, f32[3136]{0:T(1024)S(1)} %rsqrt.28, f32[3136]{0:T(1024)S(1)} %div.185), kind=kOutput, calls=%fused_computation.41 | convolution fusion | flops 3711418368 | bytes 15658496 | tf_op jit(solution)/shard_map/dot_general | solution.py:37
  409.3 15.3 %reshape.682 = bf16[16,196,12,64]{3,2,1,0:T(8,128)(2,1)} reshape(bf16[3136,768]{1,0:T(8,128)(2,1)} %convolution_convert_fusion.7) | data formatting | bytes 9633792 | tf_op jit(solution)/shard_map/reshape | solution.py:40
  424.7 30.3 %fusion.4 = (f32[16,12,196]{2,1,0:T(8,128)S(1)}, f32[16,12,196,196]{2,3,1,0:T(8,128)}) fusion(bf16[16,196,12,64]{3,2,1,0:T(8,128)(2,1)} %reshape.684, bf16[16,196,12,64]{3,2,1,0:T(8,128)(2,1)} %reshape.683), kind=kOutput, calls=%fused_computation.13 | convolution fusion | flops 958825728 | bytes 39287808 | tf_op jit(solution)/shard_map/bqhd,bkhd->bhqk/dot_general | solution.py:41
  455.0 22.3 %convert_bitcast_fusion = bf16[16,196,12,64]{1,3,2,0:T(8,128)(2,1)} fusion(f32[16,12,196,196]{2,3,1,0:T(8,128)} %get-tuple-element.23, f32[16,12,196]{2,1,0:T(8,128)S(1)} %get-tuple-element.22, bf16[16,196,12,64]{3,2,1,0:T(8,128)(2,1)} %reshape.682), kind=kOutput, calls=%fused_computation.53 | convolution fusion | flops 968647680 | bytes 39287808 | tf_op jit(solution)/shard_map/bhqk,bkhd->bqhd/dot_general | solution.py:46
  477.3 9.6 %copy.106 = bf16[16,196,12,64]{1,0,3,2:T(8,128)(2,1)} copy(bf16[16,196,12,64]{1,3,2,0:T(8,128)(2,1)} %convert_bitcast_fusion) | data formatting | bytes 9633792 | tf_op jit(solution)/shard_map/convert_element_type | solution.py:48
  486.9 12.7 %reshape.674 = bf16[3136,768]{0,1:T(8,128)(2,1)} reshape(bf16[16,196,12,64]{1,0,3,2:T(8,128)(2,1)} %copy.106) | data formatting | bytes 9633792 | tf_op jit(solution)/shard_map/reshape | solution.py:50
  499.6 8.8 %convert_reduce_fusion.1 = (f32[3136]{0:T(1024)S(1)}, bf16[3136,768]{1,0:T(8,128)(2,1)S(1)}) fusion(bf16[3136,768]{0,1:T(8,128)(2,1)} %reshape.674, bf16[768,768]{1,0:T(8,128)(2,1)S(1)} %copy-done.20, bf16[3136,768]{1,0:T(8,128)(2,1)} %copy-done.3), kind=kOutput, calls=%fused_computation.19 | convolution fusion | flops 3711415296 | bytes 15642880 | tf_op jit(solution)/shard_map/dot_general | solution.py:49
  508.4 1.5 fusion.17
  509.9 5.6 fusion.29
  515.6 4.6 copy-done.5
  520.2 2.2 fusion.78
  522.4 4.7 copy.107
  527.1 6.2 tile.4
  533.3 10.4 %copy.108 = f32[3136,768]{1,0:T(8,128)} copy(f32[3136,768]{0,1:T(8,128)} %bitcast.127) | data formatting | bytes 19267584 | tf_op jit(solution)/shard_map/tile | solution.py:65
  543.7 9.7 %fusion.21 = bf16[3136,768]{1,0:T(8,128)(2,1)} fusion(f32[3136,768]{1,0:T(8,128)} %copy.108, f32[3136,1024]{1,0:T(8,128)} %copy-done.5), kind=kLoop, calls=%fused_computation.37 | loop fusion | flops 4816896 | bytes 24084480 | tf_op jit(solution)/shard_map/convert.1
  553.4 5.1 pad_maximum_fusion.1
  558.5 7.7 slice.53
  566.2 5.3 fusion.1
  571.5 17.0 %reduce.6 = bf16[16,200704]{1,0:T(8,128)(2,1)} reduce(bf16[16,1,200704]{2,0,1:T(8,128)(2,1)} %fusion.1, bf16[]{:T(256)} %broadcast.795), dimensions={1}, to_apply=%copy.109.reduce_sub_computation | reduce | bytes 12845058 | tf_op jit(solution)/shard_map/all_to_all | solution.py:162
  588.5 9.6 %reshape.687 = bf16[16,2,100352]{2,1,0:T(2,128)(2,1)} reshape(bf16[16,200704]{1,0:T(8,128)(2,1)} %reduce.6) | data formatting | bytes 12845056
  598.2 19.2 %all-to-all-start.2 = ((bf16[16,2,100352]{2,1,0:T(2,128)(2,1)}), bf16[16,2,100352]{2,1,0:T(2,128)(2,1)}, u32[]{:S(2)}, u32[]{:S(2)}) async-start(bf16[16,2,100352]{2,1,0:T(2,128)(2,1)} %reshape.687), calls=%async_computation.2 | async-start | bytes 12845056 | tf_op jit(solution)/shard_map/all_to_all | solution.py:162
  617.4 7.7 slice.55
  625.1 6.4 convolution_convert_fusion
  631.5 7.6 all_to_all.36
  639.1 73.1 %all-to-all-done.2 = bf16[16,2,100352]{2,1,0:T(2,128)(2,1)} async-done(((bf16[16,2,100352]{2,1,0:T(2,128)(2,1)}), bf16[16,2,100352]{2,1,0:T(2,128)(2,1)}, u32[]{:S(2)}, u32[]{:S(2)}) %all-to-all-start.2) | async-done | bytes 6422560 | tf_op jit(solution)/shard_map/all_to_all | solution.py:162
  712.2 9.5 %all-to-all-start.3 = ((bf16[8,2,200704]{2,1,0:T(2,128)(2,1)}), bf16[8,2,200704]{2,1,0:T(2,128)(2,1)}, u32[]{:S(2)}, u32[]{:S(2)}) async-start(bf16[8,2,200704]{2,1,0:T(2,128)(2,1)} %all_to_all.36), calls=%async_computation.3 | async-start | bytes 12845056 | tf_op jit(solution)/shard_map/all_to_all | solution.py:163
  721.7 14.5 %reshape.688 = bf16[16,1,200704]{2,1,0:T(2,128)(2,1)} reshape(bf16[16,2,100352]{2,1,0:T(2,128)(2,1)} %all-to-all-done.2) | data formatting | bytes 12845056
  736.3 14.4 %fusion.22 = f32[8,200704]{1,0:T(8,128)} fusion(bf16[16,1,200704]{2,1,0:T(2,128)(2,1)} %reshape.688, s32[16,8]{0,1:T(8,128)S(1)} %copy-done.9), kind=kOutput, calls=%fused_computation.46 | convolution fusion | flops 51380352 | bytes 12845568 | tf_op jit(solution)/shard_map/dot_general | solution.py:164
  750.6 44.6 %all-to-all-done.3 = bf16[8,2,200704]{2,1,0:T(2,128)(2,1)} async-done(((bf16[8,2,200704]{2,1,0:T(2,128)(2,1)}), bf16[8,2,200704]{2,1,0:T(2,128)(2,1)}, u32[]{:S(2)}, u32[]{:S(2)}) %all-to-all-start.3) | async-done | bytes 6422560 | tf_op jit(solution)/shard_map/all_to_all | solution.py:163
  795.3 8.2 %fusion.2 = f32[8,200704]{1,0:T(8,128)} fusion(f32[8,200704]{1,0:T(8,128)} %fusion.22, bf16[8,2,200704]{2,1,0:T(2,128)(2,1)} %all-to-all-done.3, bf16[8,2,8]{2,1,0:T(2,128)(2,1)S(1)} %copy-done.7), kind=kOutput, calls=%fused_computation.7 | convolution fusion | flops 52985856 | bytes 19267840 | tf_op jit(solution)/shard_map/dot_general | solution.py:165
  803.5 7.4 reshape.675
  (80 shorter events, 2.1 us)
Async XLA Ops:
  0.0 509.9 %copy-start = (bf16[768,1024]{1,0:T(8,128)(2,1)S(1)}, bf16[768,1024]{1,0:T(8,128)(2,1)}, u32[]{:S(2)}) copy-start(bf16[768,1024]{1,0:T(8,128)(2,1)} %param.23) | copy-start | bytes 4718596
  55.9 14.2 %copy-start.6 = (bf16[8,2,8]{2,1,0:T(2,128)(2,1)}, bf16[8,2,8]{2,1,0:T(2,128)(2,1)S(1)}, u32[]{:S(2)}) copy-start(bf16[8,2,8]{2,1,0:T(2,128)(2,1)S(1)} %convert_element_type.136) | copy-start | bytes 772
  77.6 78.5 %all-to-all-start.1 = ((bf16[8,2,200704]{2,1,0:T(2,128)(2,1)}), bf16[8,2,200704]{2,1,0:T(2,128)(2,1)}, u32[]{:S(2)}, u32[]{:S(2)}) async-start(bf16[8,2,200704]{2,1,0:T(2,128)(2,1)} %all_to_all.31), calls=%async_computation.1 | async-start | bytes 12845056 | tf_op jit(solution)/shard_map/all_to_all | solution.py:141
  82.8 0.6 copy-start.8
  156.1 106.9 %all-to-all-start = ((bf16[16,2,100352]{2,1,0:T(2,128)(2,1)}), bf16[16,2,100352]{2,1,0:T(2,128)(2,1)}, u32[]{:S(2)}, u32[]{:S(2)}) async-start(bf16[16,2,100352]{2,1,0:T(2,128)(2,1)} %reshape.685), calls=%async_computation | async-start | bytes 12845056 | tf_op jit(solution)/shard_map/all_to_all | solution.py:140
  164.5 113.0 %copy-start.12 = (s32[8]{0:T(128)}, s32[8]{0:T(128)S(1)}, u32[]{:S(2)}) copy-start(s32[8]{0:T(128)S(1)} %get-tuple-element.18) | copy-start | bytes 100
  165.0 112.6 %copy-start.14 = (pred[8]{0:T(512)(128)(4,1)}, pred[8]{0:T(512)(128)(4,1)S(1)}, u32[]{:S(2)}) copy-start(pred[8]{0:T(512)(128)(4,1)S(1)} %broadcast_compare_fusion.1) | copy-start | bytes 28
  165.0 0.6 copy-start.10
  277.6 11.8 %copy-start.4 = (bf16[8,200704]{1,0:T(8,128)(2,1)S(1)}, bf16[8,200704]{1,0:T(8,128)(2,1)}, u32[]{:S(2)}) copy-start(bf16[8,200704]{1,0:T(8,128)(2,1)} %fusion.3) | copy-start | bytes 9633796
  292.4 13.6 %copy-start.16 = (bf16[1024,768]{1,0:T(8,128)(2,1)S(1)}, bf16[1024,768]{1,0:T(8,128)(2,1)}, u32[]{:S(2)}) copy-start(bf16[1024,768]{1,0:T(8,128)(2,1)} %param.15) | copy-start | bytes 4718596
  314.6 2.3 copy-start.3
  327.6 7.0 copy-start.1
  327.6 7.0 copy-start.2
  338.6 10.1 %copy-start.17 = (bf16[768,768]{1,0:T(8,128)(2,1)S(1)}, bf16[768,768]{1,0:T(8,128)(2,1)}, u32[]{:S(2)}) copy-start(bf16[768,768]{1,0:T(8,128)(2,1)} %param.19) | copy-start | bytes 3538948
  338.7 10.1 %copy-start.22 = (f32[768]{0:T(1024)S(1)}, f32[768]{0:T(1024)}, u32[]{:S(2)}) copy-start(f32[768]{0:T(1024)} %param.17) | copy-start | bytes 9220
  357.7 19.3 %copy-start.18 = (bf16[768,768]{1,0:T(8,128)(2,1)S(1)}, bf16[768,768]{1,0:T(8,128)(2,1)}, u32[]{:S(2)}) copy-start(bf16[768,768]{1,0:T(8,128)(2,1)} %param.18) | copy-start | bytes 3538948
  357.7 19.3 %copy-start.21 = (f32[768]{0:T(1024)S(1)}, f32[768]{0:T(1024)}, u32[]{:S(2)}) copy-start(f32[768]{0:T(1024)} %param.16) | copy-start | bytes 9220
  385.1 15.5 %copy-start.19 = (bf16[768,768]{1,0:T(8,128)(2,1)S(1)}, bf16[768,768]{1,0:T(8,128)(2,1)}, u32[]{:S(2)}) copy-start(bf16[768,768]{1,0:T(8,128)(2,1)} %param.20) | copy-start | bytes 3538948
  486.9 12.7 %copy-start.20 = (bf16[768,768]{1,0:T(8,128)(2,1)S(1)}, bf16[768,768]{1,0:T(8,128)(2,1)}, u32[]{:S(2)}) copy-start(bf16[768,768]{1,0:T(8,128)(2,1)} %param.21) | copy-start | bytes 3538948
  499.6 10.3 %copy-start.23 = (f32[768]{0:T(1024)S(1)}, f32[768]{0:T(1024)}, u32[]{:S(2)}) copy-start(f32[768]{0:T(1024)} %param.22) | copy-start | bytes 9220
  515.6 4.6 copy-start.5
  558.5 7.7 copy-start.13
  558.5 7.7 copy-start.15
  598.2 19.2 %copy-start.11 = (pred[8,8,2]{0,2,1:T(4,128)(4,1)S(1)}, pred[8,8,2]{0,2,1:T(4,128)(4,1)}, u32[]{:S(2)}) copy-start(pred[8,8,2]{0,2,1:T(4,128)(4,1)} %copy-done.10) | copy-start | bytes 388
  598.2 114.0 %all-to-all-start.2 = ((bf16[16,2,100352]{2,1,0:T(2,128)(2,1)}), bf16[16,2,100352]{2,1,0:T(2,128)(2,1)}, u32[]{:S(2)}, u32[]{:S(2)}) async-start(bf16[16,2,100352]{2,1,0:T(2,128)(2,1)} %reshape.687), calls=%async_computation.2 | async-start | bytes 12845056 | tf_op jit(solution)/shard_map/all_to_all | solution.py:162
  712.2 83.1 %all-to-all-start.3 = ((bf16[8,2,200704]{2,1,0:T(2,128)(2,1)}), bf16[8,2,200704]{2,1,0:T(2,128)(2,1)}, u32[]{:S(2)}, u32[]{:S(2)}) async-start(bf16[8,2,200704]{2,1,0:T(2,128)(2,1)} %all_to_all.36), calls=%async_computation.3 | async-start | bytes 12845056 | tf_op jit(solution)/shard_map/all_to_all | solution.py:163
  721.7 14.6 %copy-start.9 = (s32[16,8]{0,1:T(8,128)S(1)}, s32[16,8]{0,1:T(8,128)}, u32[]{:S(2)}) copy-start(s32[16,8]{0,1:T(8,128)} %copy-done.8) | copy-start | bytes 1540
  736.3 59.0 %copy-start.7 = (bf16[8,2,8]{2,1,0:T(2,128)(2,1)S(1)}, bf16[8,2,8]{2,1,0:T(2,128)(2,1)}, u32[]{:S(2)}) copy-start(bf16[8,2,8]{2,1,0:T(2,128)(2,1)} %copy-done.6) | copy-start | bytes 772
where the time goes:
time: 821 us; the launch traced here: 811 us
  waiting for transfers between devices  249 us (30%)
  local copies, waits for them, and re-layouts  227 us (28%)
  matrix products  166 us (20%)
  other arithmetic  72.3 us (9%)
  blocking collectives  54.3 us (7%)
  starting transfers between devices  42 us (5%)
    all_to_all x1, waiting for transfers between devices, per_device(): lax.all_to_all(send_first, 'gy', split_axis=0, concat_axis=0, tiled=True)  90.8 us
    all_to_all x1, waiting for transfers between devices, per_device(): lax.all_to_all(back_first, 'gy', split_axis=0, concat_axis=0, tiled=True)  73.1 us
    unnamed x53, local copies, waits for them, and re-layouts  56.4 us
    all_gather x1, blocking collectives, per_device(): lax.all_gather(slots, ('gx', 'gy'), axis=0, tiled=True)  54.3 us
    all_to_all x1, waiting for transfers between devices, per_device(): lax.all_to_all(back_second, 'gx', split_axis=0, concat_axis=0, tiled=True)  44.6 us
    all_to_all x1, waiting for transfers between devices, per_device(): lax.all_to_all(send_second, 'gx', split_axis=0, concat_axis=0, tiled=True)  40.6 us
    dot_general x1, matrix products, cross_block(): jnp.einsum('bqhd,bkhd->bhqk', query_proj, key_proj, preferred_element_typ...  30.3 us
    dot_general x1, matrix products, cross_block(): jnp.einsum('bhqk,bkhd->bqhd', weights, value_proj, preferred_element_type...  22.3 us
  transfers between devices with their start and end apart: 4, of which 4 were waited for; matrix products, arithmetic and copies ran while one was open for 10% of the time, Pallas kernels for 0%

commit v1 on v0

v1 whole, which is shorter than its diff:
```python
import functools

import jax
import jax.numpy as jnp
from jax import lax
from jax.experimental import pallas as pl
from jax.experimental.pallas import tpu as pltpu
from jax.sharding import PartitionSpec as P

D_ENC = 1024
D_MODEL = 768
HEADS = 12
PATCHES = 196
PIXELS = 256
HEAD_OUT = 1024
IMG_DEV = 8
PAIR_DEV = 8
N_GX = 8
N_GY = 16
SLOTS = 32
SIZES = (48, 48, 48, 52)
PARTS = len(SIZES)
STARTS = tuple(sum(SIZES[:part]) for part in range(PARTS))
PADDED = tuple(-(-size // 16) * 16 for size in SIZES)
ROWS = STARTS[-1] + PADDED[-1]
MESH = pl.DeviceIdType.MESH
BF16 = jnp.bfloat16
F32 = jnp.float32


def ring_distance(step):
    return min(step, 4 - step)


GY_STEPS = sorted(
    [(dx, dy) for dx in range(4) for dy in range(4) if (dx, dy) != (0, 0)],
    key=lambda step: -(ring_distance(step[0]) + ring_distance(step[1])),
)
GX_STEPS = sorted(range(1, N_GX), key=lambda step: -ring_distance(step // 2))


def normalize(values):
    mean = jnp.mean(values, axis=-1, keepdims=True)
    centered = values - mean
    spread = jnp.mean(centered * centered, axis=-1, keepdims=True)
    return centered * lax.rsqrt(spread + 1e-06)


def exchange_kernel(
    image_slot,
    pairs,
    tokens_hbm,
    w_embed_hbm,
    gain_query,
    gain_key,
    w_query_hbm,
    w_key_hbm,
    w_value_hbm,
    w_out_hbm,
    *refs,
):
    back, (table_out,), refs = refs[:PARTS], refs[PARTS : PARTS + 1], refs[PARTS + 1 :]
    send, recv, refs = refs[:PARTS], refs[PARTS : 2 * PARTS], refs[2 * PARTS :]
    (
    tokens,
    w_embed,
    w_query,
    w_key,
    w_value,
    w_out,
    embedded,
    views,
    q_all,
    k_all,
    v_all,
    mixed,
    message,
    got_message,
    lists,
    source,
    inverse,
    load_sem,
    list_sem,
    self_sem,
    msg_send,
    msg_recv,
    fwd_send,
    fwd_recv,
    bwd_send,
    bwd_recv,
    ) = refs
    gx = lax.axis_index("gx")
    gy = lax.axis_index("gy")

    loads = [
        pltpu.make_async_copy(src, dst, load_sem.at[i])
        for i, (src, dst) in enumerate(
            [
                (tokens_hbm, tokens),
                (w_embed_hbm, w_embed),
                (w_query_hbm, w_query),
                (w_key_hbm, w_key),
                (w_value_hbm, w_value),
                (w_out_hbm, w_out),
            ]
        )
    ]
    for load in loads:
        load.start()

    def gy_peer(step):
        dx, dy = step
        return ((gy // 4 + dx) % 4) * 4 + (gy % 4 + dy) % 4

    def gx_peer(step):
        return ((gx // 2 + step // 2) % 4) * 2 + (gx % 2 + step % 2) % 2

    barrier = pltpu.get_barrier_semaphore()
    for step in GY_STEPS:
        pl.semaphore_signal(barrier, inc=1, device_id=(gx, gy_peer(step)), device_id_type=MESH)
    for step in GX_STEPS:
        pl.semaphore_signal(barrier, inc=1, device_id=(gx_peer(step), gy), device_id_type=MESH)

    lane = lax.broadcasted_iota(jnp.int32, (8, 128), 1)
    row = jnp.zeros((8, 128), jnp.int32)
    own = []
    for p in range(PAIR_DEV):
        for s in range(2):
            value = image_slot[pairs[p, s]]
            own.append(value)
            row = jnp.where(lane == 2 * p + s, value, row)
    message[...] = row
    got_message[gy] = row
    got_message[N_GY + gx] = row
    pl.semaphore_wait(barrier, N_GY - 1 + N_GX - 1)

    def message_copy(place, sender, device):
        return pltpu.make_async_remote_copy(
            src_ref=message,
            dst_ref=got_message.at[sender],
            send_sem=msg_send.at[place],
            recv_sem=msg_recv.at[sender],
            device_id=device,
            device_id_type=MESH,
        )

    for step in GY_STEPS:
        peer = gy_peer(step)
        message_copy(peer, gy, (gx, peer)).start()
    for step in GX_STEPS:
        peer = gx_peer(step)
        message_copy(N_GY + peer, N_GY + gx, (peer, gy)).start()

    cols = [(own[2 * p] // IMG_DEV) % N_GY for p in range(PAIR_DEV)]
    rows = [own[2 * p + 1] // (IMG_DEV * N_GY) for p in range(PAIR_DEV)]
    places = []
    for p in range(PAIR_DEV):
        rank = jnp.int32(0)
        for earlier in range(p):
            rank = rank + (rows[earlier] == rows[p]).astype(jnp.int32)
        places.append(N_GY + 2 * rows[p] + rank)
        source[p] = cols[p]
        source[PAIR_DEV + p] = places[p]
    for slot in range(SLOTS):
        view = jnp.int32(0)
        for p in range(PAIR_DEV):
            if slot < N_GY:
                view = jnp.where(cols[p] == slot, p, view)
            else:
                view = jnp.where(places[p] == slot, PAIR_DEV + p, view)
        inverse[slot] = view

    loads[0].wait()
    loads[1].wait()
    half = 4 * PATCHES
    for part in range(2):
        value = jnp.dot(
            tokens[part * half : (part + 1) * half], w_embed[...], preferred_element_type=F32
        )
        for i in range(4):
            embedded[part * 4 + i, :PATCHES] = value[i * PATCHES : (i + 1) * PATCHES].astype(BF16)

    for step in GY_STEPS:
        peer = gy_peer(step)
        copy = message_copy(peer, peer, (gx, peer))
        copy.wait_send()
        copy.wait_recv()
    for step in GX_STEPS:
        peer = gx_peer(step)
        copy = message_copy(N_GY + peer, N_GY + peer, (peer, gy))
        copy.wait_send()
        copy.wait_recv()
    to_lists = pltpu.make_async_copy(got_message, lists, list_sem)
    to_lists.start()
    to_lists.wait()

    def find_first(worker, carry):
        image = jnp.int32(0)
        valid = jnp.int32(0)
        for p in range(PAIR_DEV):
            slot = lists[worker, 0, 2 * p]
            hit = (slot // IMG_DEV) % N_GY == gy
            image = jnp.where(hit, slot % IMG_DEV, image)
            valid = jnp.where(hit, 1, valid)
        table_out[worker] = image
        table_out[SLOTS + worker] = valid
        return carry

    def find_second(worker, carry):
        image = [jnp.int32(0), jnp.int32(0)]
        found = jnp.int32(0)
        for p in range(PAIR_DEV):
            slot = lists[N_GY + worker, 0, 2 * p + 1]
            hit = slot // (IMG_DEV * N_GY) == gx
            for j in range(2):
                image[j] = jnp.where(hit & (found == j), slot % IMG_DEV, image[j])
            found = found + hit.astype(jnp.int32)
        for j in range(2):
            table_out[N_GY + 2 * worker + j] = image[j]
            table_out[SLOTS + N_GY + 2 * worker + j] = jnp.where(found > j, 1, 0)
        return carry

    lax.fori_loop(0, N_GY, find_first, 0)
    lax.fori_loop(0, N_GX, find_second, 0)

    def slot_copies(part, forward):
        target = recv[part] if forward else back[part]
        sent, received = (fwd_send, fwd_recv) if forward else (bwd_send, bwd_recv)

        def gy_copy(peer, sender):
            return pltpu.make_async_remote_copy(
                src_ref=send[part].at[peer],
                dst_ref=target.at[sender],
                send_sem=sent.at[part, peer],
                recv_sem=received.at[part, sender],
                device_id=(gx, peer),
                device_id_type=MESH,
            )

        def gx_copy(peer, sender):
            return pltpu.make_async_remote_copy(
                src_ref=send[part].at[pl.ds(N_GY + 2 * peer, 2)],
                dst_ref=target.at[pl.ds(N_GY + 2 * sender, 2)],
                send_sem=sent.at[part, N_GY + peer],
                recv_sem=received.at[part, N_GY + sender],
                device_id=(peer, gy),
                device_id_type=MESH,
            )

        return gy_copy, gx_copy

    def start_copies(part, forward):
        gy_copy, gx_copy = slot_copies(part, forward)
        for i in range(max(len(GY_STEPS), len(GX_STEPS))):
            gy_copy(gy_peer(GY_STEPS[i]), gy).start()
            if i < len(GX_STEPS):
                gx_copy(gx_peer(GX_STEPS[i]), gx).start()

    def wait_copies(part, forward, what):
        gy_copy, gx_copy = slot_copies(part, forward)

        def wait(copy):
            if what == "send":
                copy.wait_send()
            else:
                copy.wait_recv()

        for step in GY_STEPS:
            peer = gy_peer(step)
            wait(gy_copy(peer, peer))
        for step in GX_STEPS:
            peer = gx_peer(step)
            wait(gx_copy(peer, peer))

    for part in range(PARTS):
        exact = slice(STARTS[part], STARTS[part] + SIZES[part])

        def pack(slot, carry):
            send[part][slot] = embedded[table_out[slot], exact]
            return carry

        lax.fori_loop(0, SLOTS, pack, 0)
        start_copies(part, True)
        for slot in (gy, N_GY + 2 * gx, N_GY + 2 * gx + 1):
            recv[part][slot] = embedded[table_out[slot], exact]
    for load in loads[2:]:
        load.wait()
    views[:, STARTS[-1] :] = jnp.zeros((2 * PAIR_DEV, PADDED[-1], D_MODEL), BF16)

    def project(part):
        wait_copies(part, True, "recv")
        size = PADDED[part]
        exact = slice(STARTS[part], STARTS[part] + SIZES[part])
        place = slice(STARTS[part], STARTS[part] + size)

        def side(group, carry):
            for p in range(PAIR_DEV):
                view = group * PAIR_DEV + p
                views[view, exact] = recv[part][source[view]]
            block = jnp.concatenate(
                [views[group * PAIR_DEV + p, place] for p in range(PAIR_DEV)], axis=0
            ).astype(F32)
            normal = normalize(block)
            normed_q = (normal * gain_query[...]).astype(BF16)
            normed_k = (normal * gain_key[...]).astype(BF16)
            for normed, weight, out, scale in (
                (normed_q, w_query, q_all, (D_MODEL // HEADS) ** -0.5),
                (normed_k, w_key, k_all, None),
                (normed_k, w_value, v_all, None),
            ):
                value = jnp.dot(normed, weight[...], preferred_element_type=F32)
                if scale is not None:
                    value = value * scale
                value = value.astype(BF16)
                for p in range(PAIR_DEV):
                    out[group * PAIR_DEV + p, place] = value[p * size : (p + 1) * size]
            return carry

        lax.fori_loop(0, 2, side, 0)

    for part in range(PARTS):
        project(part)
    for part in range(PARTS):
        wait_copies(part, True, "send")

    def attend(part):
        size = PADDED[part]
        exact = slice(STARTS[part], STARTS[part] + SIZES[part])
        place = slice(STARTS[part], STARTS[part] + size)
        quad = 4 * (D_MODEL // HEADS)
        head_of = lax.broadcasted_iota(jnp.int32, (size, quad), 1) // (D_MODEL // HEADS)
        key_of = lax.broadcasted_iota(jnp.int32, (4 * size, ROWS), 1)

        def one_view(view, carry):
            other = (view + PAIR_DEV) % (2 * PAIR_DEV)
            for four in range(HEADS // 4):
                features = slice(four * quad, (four + 1) * quad)
                query = q_all[view, place, features]
                stacked = jnp.concatenate(
                    [jnp.where(head_of == j, query, jnp.zeros_like(query)) for j in range(4)], axis=0
                )
                scores = lax.dot_general(
                    stacked,
                    k_all[other, :, features],
                    (((1,), (1,)), ((), ())),
                    preferred_element_type=F32,
                )
                scores = jnp.where(key_of < PATCHES, scores, -jnp.inf)
                expd = jnp.exp(scores - jnp.max(scores, axis=-1, keepdims=True))
                weights = (expd * (1.0 / jnp.sum(expd, axis=-1, keepdims=True))).astype(BF16)
                out = jnp.dot(weights, v_all[other, :, features], preferred_element_type=F32)
                attended = out[:size]
                for j in range(1, 4):
                    attended = jnp.where(head_of == j, out[j * size : (j + 1) * size], attended)
                mixed[view, :size, features] = attended.astype(BF16)
            return carry

        lax.fori_loop(0, 2 * PAIR_DEV, one_view, 0)

        def side(group, carry):
            block = jnp.concatenate(
                [mixed[group * PAIR_DEV + p, :size] for p in range(PAIR_DEV)], axis=0
            )
            value = jnp.dot(block, w_out[...], preferred_element_type=F32)
            for p in range(PAIR_DEV):
                view = group * PAIR_DEV + p
                query = views[view, place].astype(F32)
                views[view, place] = (query + value[p * size : (p + 1) * size]).astype(BF16)
            return carry

        lax.fori_loop(0, 2, side, 0)

        def pack(slot, carry):
            send[part][slot] = views[inverse[slot], exact]
            return carry

        lax.fori_loop(0, SLOTS, pack, 0)
        start_copies(part, False)
        for copy in self_copies(part):
            copy.start()

    def self_copies(part):
        return [
            pltpu.make_async_copy(send[part].at[place], back[part].at[place], self_sem.at[part, i])
            for i, place in enumerate([pl.ds(gy, 1), pl.ds(N_GY + 2 * gx, 2)])
        ]

    for part in range(PARTS):
        attend(part)
    for part in range(PARTS):
        for copy in self_copies(part):
            copy.wait()
        wait_copies(part, False, "send")
        wait_copies(part, False, "recv")


def exchange(image_slot, pairs, tokens, w_embed, gain_query, gain_key, w_query, w_key, w_value, w_out):
    any_space = pl.BlockSpec(memory_space=pl.ANY)
    smem = pl.BlockSpec(memory_space=pltpu.SMEM)
    vmem = pl.BlockSpec(memory_space=pltpu.VMEM)
    square = pltpu.VMEM((D_MODEL, D_MODEL), BF16)
    full = pltpu.VMEM((2 * PAIR_DEV, ROWS, D_MODEL), BF16)
    return pl.pallas_call(
        exchange_kernel,
        out_shape=[jax.ShapeDtypeStruct((SLOTS, size, D_MODEL), BF16) for size in SIZES]
        + [jax.ShapeDtypeStruct((2 * SLOTS,), jnp.int32)],
        in_specs=[smem, smem, any_space, any_space, vmem, vmem] + [any_space] * 4,
        out_specs=[any_space] * PARTS + [smem],
        scratch_shapes=[pltpu.VMEM((SLOTS, size, D_MODEL), BF16) for size in SIZES * 2]
        + [
            pltpu.VMEM((IMG_DEV * PATCHES, D_ENC), BF16),
            pltpu.VMEM((D_ENC, D_MODEL), BF16),
            square,
            square,
            square,
            square,
            pltpu.VMEM((IMG_DEV, ROWS, D_MODEL), BF16),
            full,
            full,
            full,
            full,
            pltpu.VMEM((2 * PAIR_DEV, max(PADDED), D_MODEL), BF16),
            pltpu.VMEM((8, 128), jnp.int32),
            pltpu.VMEM((N_GY + N_GX, 8, 128), jnp.int32),
            pltpu.SMEM((N_GY + N_GX, 8, 128), jnp.int32),
            pltpu.SMEM((2 * PAIR_DEV,), jnp.int32),
            pltpu.SMEM((SLOTS,), jnp.int32),
            pltpu.SemaphoreType.DMA((6,)),
            pltpu.SemaphoreType.DMA,
            pltpu.SemaphoreType.DMA((PARTS, 2)),
            pltpu.SemaphoreType.DMA((N_GY + N_GX,)),
            pltpu.SemaphoreType.DMA((N_GY + N_GX,)),
            pltpu.SemaphoreType.DMA((PARTS, N_GY + N_GX)),
            pltpu.SemaphoreType.DMA((PARTS, N_GY + N_GX)),
            pltpu.SemaphoreType.DMA((PARTS, N_GY + N_GX)),
            pltpu.SemaphoreType.DMA((PARTS, N_GY + N_GX)),
        ],
        compiler_params=pltpu.CompilerParams(
            collective_id=0, has_side_effects=True, vmem_limit_bytes=62 * 2**20
        ),
        name="exchange",
    )(image_slot, pairs, tokens, w_embed, gain_query, gain_key, w_query, w_key, w_value, w_out)


def head_kernel(table, *refs):
    sources, (gain, w_head, out), refs = refs[:PARTS], refs[PARTS : PARTS + 3], refs[PARTS + 3 :]
    blocks, (joined, total, order, sems) = refs[:PARTS], refs[PARTS:]

    def collect(slot, count):
        order[count] = slot
        return count + table[SLOTS + slot]

    count = lax.fori_loop(0, SLOTS, collect, jnp.int32(0))

    def copies(item):
        slot = order[item]
        place = item % 2
        return [
            pltpu.make_async_copy(sources[part].at[slot], blocks[part].at[place], sems.at[part, place])
            for part in range(PARTS)
        ]

    @pl.when(count > 0)
    def _():
        for copy in copies(0):
            copy.start()

    total[...] = jnp.zeros_like(total)
    joined[STARTS[-1] :] = jnp.zeros((PADDED[-1], D_MODEL), BF16)

    def step(item, carry):
        @pl.when(item + 1 < count)
        def _():
            for copy in copies(item + 1):
                copy.start()

        for copy in copies(item):
            copy.wait()
        place = item % 2
        image = table[order[item]]
        for start, size, ref in zip(STARTS, SIZES, blocks):
            joined[start : start + size] = ref[place]
        normed = (normalize(joined[...].astype(F32)) * gain[...]).astype(BF16)
        raw = jnp.dot(normed, w_head[...], preferred_element_type=F32)
        confidence = 1.0 + jnp.exp(raw[:, 3 * PIXELS :])
        for plane in range(4):
            columns = slice(plane * PIXELS, (plane + 1) * PIXELS)
            value = confidence if plane == 3 else raw[:, columns] * confidence
            total[image, :, columns] += value.astype(BF16).astype(F32)
        return carry

    lax.fori_loop(0, count, step, 0)
    for image in range(IMG_DEV):
        out[image * PATCHES : (image + 1) * PATCHES] = total[image, :PATCHES]


def head(table, parts, gain, w_head):
    any_space = pl.BlockSpec(memory_space=pl.ANY)
    vmem = pl.BlockSpec(memory_space=pltpu.VMEM)
    return pl.pallas_call(
        head_kernel,
        out_shape=jax.ShapeDtypeStruct((IMG_DEV * PATCHES, HEAD_OUT), F32),
        in_specs=[pl.BlockSpec(memory_space=pltpu.SMEM), *[any_space] * PARTS, vmem, vmem],
        out_specs=vmem,
        scratch_shapes=[pltpu.VMEM((2, size, D_MODEL), BF16) for size in SIZES]
        + [
            pltpu.VMEM((ROWS, D_MODEL), BF16),
            pltpu.VMEM((IMG_DEV, ROWS, HEAD_OUT), F32),
            pltpu.SMEM((SLOTS + 1,), jnp.int32),
            pltpu.SemaphoreType.DMA((PARTS, 2)),
        ],
        compiler_params=pltpu.CompilerParams(vmem_limit_bytes=60 * 2**20),
        name="head",
    )(table, *parts, gain, w_head)


def per_device(
    tokens,
    image_slot,
    pairs,
    w_embed,
    gain_query,
    gain_key,
    w_query,
    w_key,
    w_value,
    w_out,
    gain_head,
    w_head,
):
    *parts, table = exchange(
        image_slot,
        pairs,
        tokens,
        w_embed,
        gain_query.reshape(1, D_MODEL),
        gain_key.reshape(1, D_MODEL),
        w_query,
        w_key,
        w_value,
        w_out,
    )
    return head(table, parts, gain_head.reshape(1, D_MODEL), w_head)


def solution(mesh):
    split = P(("gx", "gy"), None)
    return jax.shard_map(
        per_device,
        mesh=mesh,
        in_specs=(split, P(), split) + (P(),) * 9,
        out_specs=split,
        check_vma=False,
    )
```

time: 821 us -> 204 us (0.25)
  the two profiles are of different devices: /device:TPU:20 before, /device:TPU:34 now
where the time goes in v1:
time: 204 us; the launch traced here: 203 us
  Pallas kernels  198 us (97%)
  local copies, waits for them, and re-layouts  5.18 us (3%)
    pallas_call x1, Pallas kernels, exchange(): pl.pallas_call(exchange_kernel, out_shape=[jax.ShapeDtypeStruct((SLOTS, s...  169 us
    pallas_call x1, Pallas kernels, head(): pl.pallas_call(head_kernel, out_shape=jax.ShapeDtypeStruct((IMG_DEV * PAT...  28.3 us

profile of v1, /device:TPU:34, one launch (start us, length us, event | category | flops | bytes accessed | tf_op | source)
XLA Modules:
  0.0 203.1 jit_solution(13942209064778139421)
XLA Ops:
  0.0 1.3 reshape.9.gain_query
  1.3 1.3 reshape.10.gain_key
  2.6 1.3 reshape.11.refs_4_
  3.8 1.3 copy.13.pairs
  5.2 169.4 %exchange.1 = (bf16[32,48,768]{2,1,0:T(8,128)(2,1)}, bf16[32,48,768]{2,1,0:T(8,128)(2,1)}, bf16[32,48,768]{2,1,0:T(8,128)(2,1)}, bf16[32,52,768]{2,1,0:T(8,128)(2,1)}, s32[64]{0:T(128)}) custom-call(s32[1024]{0:T(1024)} %image_slot.1, s32[8,2]{1,0:T(8,128)} %copy.13.pairs, bf16[1568,1024]{1,0:T(8,128)(2,1)} %tokens_hbm.1, bf16[1024,768]{1,0:T(8,128)(2,1)} %w_embed_hbm.1, ...), custom_call_target="tpu_custom_call" | custom-call | tf_op jit(solution)/shard_map/exchange/pallas_call | solution.py:403
  174.6 28.3 %head.1 = f32[1568,1024]{1,0:T(8,128)} custom-call(s32[64]{0:T(128)} %get-tuple-element.10.table, bf16[32,48,768]{2,1,0:T(8,128)(2,1)} %get-tuple-element.11.refs_0_, bf16[32,48,768]{2,1,0:T(8,128)(2,1)} %get-tuple-element.12.refs_1_, bf16[32,48,768]{2,1,0:T(8,128)(2,1)} %get-tuple-element.13.refs_2_, bf16[32,52,768]{2,1,0:T(8,128)(2,1)} %get-tuple-element.14.refs_3_, ...), custom_call_target="tpu_custom_call" | custom-call | tf_op jit(solution)/shard_map/head/pallas_call | solution.py:500

commit v2 on v1

--- a/solution.py
+++ b/solution.py
@@ -18,7 +18,11 @@
 N_GX = 8
 N_GY = 16
 SLOTS = 32
+HEAD_GROUP = 4
+GROUP = 4
 SIZES = (48, 48, 48, 52)
+OUTWARD = (0, 1, 2, 3)
+HOMEWARD = (0, 1, 2, 3)
 PARTS = len(SIZES)
 STARTS = tuple(sum(SIZES[:part]) for part in range(PARTS))
 PADDED = tuple(-(-size // 16) * 16 for size in SIZES)
@@ -53,6 +57,7 @@
     w_embed_hbm,
     gain_query,
     gain_key,
+    gain_head,
     w_query_hbm,
     w_key_hbm,
     w_value_hbm,
@@ -78,7 +83,7 @@
     got_message,
     lists,
     source,
-    inverse,
+    asks,
     load_sem,
     list_sem,
     self_sem,
@@ -121,17 +126,29 @@
     for step in GX_STEPS:
         pl.semaphore_signal(barrier, inc=1, device_id=(gx_peer(step), gy), device_id_type=MESH)
 
-    lane = lax.broadcasted_iota(jnp.int32, (8, 128), 1)
-    row = jnp.zeros((8, 128), jnp.int32)
-    own = []
+    lane = lax.broadcasted_iota(jnp.int32, (1, 128), 1)
+    asked = jnp.zeros((1, 128), jnp.int32)
+    inverse = jnp.zeros((1, 128), jnp.int32)
+    rows = []
     for p in range(PAIR_DEV):
-        for s in range(2):
-            value = image_slot[pairs[p, s]]
-            own.append(value)
-            row = jnp.where(lane == 2 * p + s, value, row)
-    message[...] = row
-    got_message[gy] = row
-    got_message[N_GY + gx] = row
+        first = image_slot[pairs[0, p]]
+        second = image_slot[pairs[1, p]]
+        row = second // (IMG_DEV * N_GY)
+        rank = jnp.int32(0)
+        for earlier in rows:
+            rank = rank + jnp.where(earlier == row, 1, 0)
+        rows.append(row)
+        for view, slot, value in (
+            (p, (first // IMG_DEV) % N_GY, first),
+            (PAIR_DEV + p, N_GY + 2 * row + rank, second),
+        ):
+            source[view] = slot
+            asked = jnp.where(lane == slot, IMG_DEV + value % IMG_DEV, asked)
+            inverse = jnp.where(lane == slot, view, inverse)
+    message[...] = asked
+    got_message[gy] = asked
+    got_message[N_GY + gx] = asked
+    got_message[N_GY + N_GX] = inverse
     pl.semaphore_wait(barrier, N_GY - 1 + N_GX - 1)
 
     def message_copy(place, sender, device):
@@ -150,25 +167,6 @@
     for step in GX_STEPS:
         peer = gx_peer(step)
         message_copy(N_GY + peer, N_GY + gx, (peer, gy)).start()
-
-    cols = [(own[2 * p] // IMG_DEV) % N_GY for p in range(PAIR_DEV)]
-    rows = [own[2 * p + 1] // (IMG_DEV * N_GY) for p in range(PAIR_DEV)]
-    places = []
-    for p in range(PAIR_DEV):
-        rank = jnp.int32(0)
-        for earlier in range(p):
-            rank = rank + (rows[earlier] == rows[p]).astype(jnp.int32)
-        places.append(N_GY + 2 * rows[p] + rank)
-        source[p] = cols[p]
-        source[PAIR_DEV + p] = places[p]
-    for slot in range(SLOTS):
-        view = jnp.int32(0)
-        for p in range(PAIR_DEV):
-            if slot < N_GY:
-                view = jnp.where(cols[p] == slot, p, view)
-            else:
-                view = jnp.where(places[p] == slot, PAIR_DEV + p, view)
-        inverse[slot] = view
 
     loads[0].wait()
     loads[1].wait()
@@ -194,34 +192,13 @@
     to_lists.start()
     to_lists.wait()
 
-    def find_first(worker, carry):
-        image = jnp.int32(0)
-        valid = jnp.int32(0)
-        for p in range(PAIR_DEV):
-            slot = lists[worker, 0, 2 * p]
-            hit = (slot // IMG_DEV) % N_GY == gy
-            image = jnp.where(hit, slot % IMG_DEV, image)
-            valid = jnp.where(hit, 1, valid)
-        table_out[worker] = image
-        table_out[SLOTS + worker] = valid
-        return carry
-
-    def find_second(worker, carry):
-        image = [jnp.int32(0), jnp.int32(0)]
-        found = jnp.int32(0)
-        for p in range(PAIR_DEV):
-            slot = lists[N_GY + worker, 0, 2 * p + 1]
-            hit = slot // (IMG_DEV * N_GY) == gx
-            for j in range(2):
-                image[j] = jnp.where(hit & (found == j), slot % IMG_DEV, image[j])
-            found = found + hit.astype(jnp.int32)
-        for j in range(2):
-            table_out[N_GY + 2 * worker + j] = image[j]
-            table_out[SLOTS + N_GY + 2 * worker + j] = jnp.where(found > j, 1, 0)
-        return carry
-
-    lax.fori_loop(0, N_GY, find_first, 0)
-    lax.fori_loop(0, N_GX, find_second, 0)
+    for slot in range(SLOTS):
+        if slot < N_GY:
+            value = lists[slot, 0, gy]
+        else:
+            value = lists[N_GY + (slot - N_GY) // 2, 0, N_GY + 2 * gx + slot % 2]
+        asks[slot] = value % IMG_DEV
+        table_out[slot] = value
 
     def slot_copies(part, forward):
         target = recv[part] if forward else back[part]
@@ -272,17 +249,17 @@
             peer = gx_peer(step)
             wait(gx_copy(peer, peer))
 
-    for part in range(PARTS):
+    for part in OUTWARD:
         exact = slice(STARTS[part], STARTS[part] + SIZES[part])
 
         def pack(slot, carry):
-            send[part][slot] = embedded[table_out[slot], exact]
+            send[part][slot] = embedded[asks[slot], exact]
             return carry
 
         lax.fori_loop(0, SLOTS, pack, 0)
         start_copies(part, True)
         for slot in (gy, N_GY + 2 * gx, N_GY + 2 * gx + 1):
-            recv[part][slot] = embedded[table_out[slot], exact]
+            recv[part][slot] = embedded[asks[slot], exact]
     for load in loads[2:]:
         load.wait()
     views[:, STARTS[-1] :] = jnp.zeros((2 * PAIR_DEV, PADDED[-1], D_MODEL), BF16)
@@ -318,7 +295,7 @@
 
         lax.fori_loop(0, 2, side, 0)
 
-    for part in range(PARTS):
+    for part in OUTWARD:
         project(part)
     for part in range(PARTS):
         wait_copies(part, True, "send")
@@ -331,31 +308,46 @@
         head_of = lax.broadcasted_iota(jnp.int32, (size, quad), 1) // (D_MODEL // HEADS)
         key_of = lax.broadcasted_iota(jnp.int32, (4 * size, ROWS), 1)
 
-        def one_view(view, carry):
-            other = (view + PAIR_DEV) % (2 * PAIR_DEV)
-            for four in range(HEADS // 4):
-                features = slice(four * quad, (four + 1) * quad)
-                query = q_all[view, place, features]
-                stacked = jnp.concatenate(
-                    [jnp.where(head_of == j, query, jnp.zeros_like(query)) for j in range(4)], axis=0
-                )
-                scores = lax.dot_general(
-                    stacked,
-                    k_all[other, :, features],
-                    (((1,), (1,)), ((), ())),
-                    preferred_element_type=F32,
-                )
-                scores = jnp.where(key_of < PATCHES, scores, -jnp.inf)
-                expd = jnp.exp(scores - jnp.max(scores, axis=-1, keepdims=True))
-                weights = (expd * (1.0 / jnp.sum(expd, axis=-1, keepdims=True))).astype(BF16)
-                out = jnp.dot(weights, v_all[other, :, features], preferred_element_type=F32)
-                attended = out[:size]
-                for j in range(1, 4):
-                    attended = jnp.where(head_of == j, out[j * size : (j + 1) * size], attended)
-                mixed[view, :size, features] = attended.astype(BF16)
+        def score(view, features):
+            query = q_all[view, place, features]
+            stacked = jnp.concatenate(
+                [jnp.where(head_of == j, query, jnp.zeros_like(query)) for j in range(4)], axis=0
+            )
+            return lax.dot_general(
+                stacked,
+                k_all[(view + PAIR_DEV) % (2 * PAIR_DEV), :, features],
+                (((1,), (1,)), ((), ())),
+                preferred_element_type=F32,
+            )
+
+        def soften(scores):
+            scores = jnp.where(key_of < PATCHES, scores, -jnp.inf)
+            expd = jnp.exp(scores - jnp.max(scores, axis=-1, keepdims=True))
+            return (expd * (1.0 / jnp.sum(expd, axis=-1, keepdims=True))).astype(BF16)
+
+        def gather(view, features, weights):
+            out = jnp.dot(
+                weights,
+                v_all[(view + PAIR_DEV) % (2 * PAIR_DEV), :, features],
+                preferred_element_type=F32,
+            )
+            attended = out[:size]
+            for j in range(1, 4):
+                attended = jnp.where(head_of == j, out[j * size : (j + 1) * size], attended)
+            mixed[view, :size, features] = attended.astype(BF16)
+
+        def some_views(group, carry):
+            items = [
+                (group * GROUP + i, slice(four * quad, (four + 1) * quad))
+                for i in range(GROUP)
+                for four in range(HEADS // 4)
+            ]
+            weights = [soften(scores) for scores in [score(*item) for item in items]]
+            for item, weight in zip(items, weights):
+                gather(*item, weight)
             return carry
 
-        lax.fori_loop(0, 2 * PAIR_DEV, one_view, 0)
+        lax.fori_loop(0, 2 * PAIR_DEV // GROUP, some_views, 0)
 
         def side(group, carry):
             block = jnp.concatenate(
@@ -365,13 +357,14 @@
             for p in range(PAIR_DEV):
                 view = group * PAIR_DEV + p
                 query = views[view, place].astype(F32)
-                views[view, place] = (query + value[p * size : (p + 1) * size]).astype(BF16)
+                resid = (query + value[p * size : (p + 1) * size]).astype(BF16)
+                views[view, place] = (normalize(resid.astype(F32)) * gain_head[...]).astype(BF16)
             return carry
 
         lax.fori_loop(0, 2, side, 0)
 
         def pack(slot, carry):
-            send[part][slot] = views[inverse[slot], exact]
+            send[part][slot] = views[lists[N_GY + N_GX, 0, slot], exact]
             return carry
 
         lax.fori_loop(0, SLOTS, pack, 0)
@@ -385,7 +378,7 @@
             for i, place in enumerate([pl.ds(gy, 1), pl.ds(N_GY + 2 * gx, 2)])
         ]
 
-    for part in range(PARTS):
+    for part in HOMEWARD:
         attend(part)
     for part in range(PARTS):
         for copy in self_copies(part):
@@ -394,7 +387,9 @@
         wait_copies(part, False, "recv")
 
 
-def exchange(image_slot, pairs, tokens, w_embed, gain_query, gain_key, w_query, w_key, w_value, w_out):
+def exchange(
+    image_slot, pairs, tokens, w_embed, gain_query, gain_key, gain_head, w_query, w_key, w_value, w_out
+):
     any_space = pl.BlockSpec(memory_space=pl.ANY)
     smem = pl.BlockSpec(memory_space=pltpu.SMEM)
     vmem = pl.BlockSpec(memory_space=pltpu.VMEM)
@@ -403,8 +398,8 @@
     return pl.pallas_call(
         exchange_kernel,
         out_shape=[jax.ShapeDtypeStruct((SLOTS, size, D_MODEL), BF16) for size in SIZES]
-        + [jax.ShapeDtypeStruct((2 * SLOTS,), jnp.int32)],
-        in_specs=[smem, smem, any_space, any_space, vmem, vmem] + [any_space] * 4,
+        + [jax.ShapeDtypeStruct((SLOTS,), jnp.int32)],
+        in_specs=[smem, smem, any_space, any_space, vmem, vmem, vmem] + [any_space] * 4,
         out_specs=[any_space] * PARTS + [smem],
         scratch_shapes=[pltpu.VMEM((SLOTS, size, D_MODEL), BF16) for size in SIZES * 2]
         + [
@@ -420,9 +415,9 @@
             full,
             full,
             pltpu.VMEM((2 * PAIR_DEV, max(PADDED), D_MODEL), BF16),
-            pltpu.VMEM((8, 128), jnp.int32),
-            pltpu.VMEM((N_GY + N_GX, 8, 128), jnp.int32),
-            pltpu.SMEM((N_GY + N_GX, 8, 128), jnp.int32),
+            pltpu.VMEM((1, 128), jnp.int32),
+            pltpu.VMEM((N_GY + N_GX + 1, 1, 128), jnp.int32),
+            pltpu.SMEM((N_GY + N_GX + 1, 1, 128), jnp.int32),
             pltpu.SMEM((2 * PAIR_DEV,), jnp.int32),
             pltpu.SMEM((SLOTS,), jnp.int32),
             pltpu.SemaphoreType.DMA((6,)),
@@ -439,79 +434,87 @@
             collective_id=0, has_side_effects=True, vmem_limit_bytes=62 * 2**20
         ),
         name="exchange",
-    )(image_slot, pairs, tokens, w_embed, gain_query, gain_key, w_query, w_key, w_value, w_out)
+    )(image_slot, pairs, tokens, w_embed, gain_query, gain_key, gain_head, w_query, w_key, w_value, w_out)
 
 
 def head_kernel(table, *refs):
-    sources, (gain, w_head, out), refs = refs[:PARTS], refs[PARTS : PARTS + 3], refs[PARTS + 3 :]
+    sources, (w_head, out), refs = refs[:PARTS], refs[PARTS : PARTS + 2], refs[PARTS + 2 :]
     blocks, (joined, total, order, sems) = refs[:PARTS], refs[PARTS:]
 
     def collect(slot, count):
         order[count] = slot
-        return count + table[SLOTS + slot]
+        return count + jnp.where(table[slot] >= IMG_DEV, 1, 0)
 
     count = lax.fori_loop(0, SLOTS, collect, jnp.int32(0))
 
-    def copies(item):
-        slot = order[item]
-        place = item % 2
-        return [
-            pltpu.make_async_copy(sources[part].at[slot], blocks[part].at[place], sems.at[part, place])
-            for part in range(PARTS)
-        ]
-
-    @pl.when(count > 0)
+    for i in range(HEAD_GROUP - 1):
+        order[count + i] = SLOTS
+    steps = (count + HEAD_GROUP - 1) // HEAD_GROUP
+
+    def copies(step):
+        for i in range(HEAD_GROUP):
+            slot = order[step * HEAD_GROUP + i] % SLOTS
+            place = (step % 2) * HEAD_GROUP + i
+            for part in range(PARTS):
+                yield pltpu.make_async_copy(
+                    sources[part].at[slot], blocks[part].at[place], sems.at[part, place]
+                )
+
+    @pl.when(steps > 0)
     def _():
         for copy in copies(0):
             copy.start()
 
     total[...] = jnp.zeros_like(total)
-    joined[STARTS[-1] :] = jnp.zeros((PADDED[-1], D_MODEL), BF16)
-
-    def step(item, carry):
-        @pl.when(item + 1 < count)
+    for i in range(HEAD_GROUP):
+        joined[i, STARTS[-1] :] = jnp.zeros((PADDED[-1], D_MODEL), BF16)
+
+    def one_step(step, carry):
+        @pl.when(step + 1 < steps)
         def _():
-            for copy in copies(item + 1):
+            for copy in copies(step + 1):
                 copy.start()
 
-        for copy in copies(item):
+        for copy in copies(step):
             copy.wait()
-        place = item % 2
-        image = table[order[item]]
-        for start, size, ref in zip(STARTS, SIZES, blocks):
-            joined[start : start + size] = ref[place]
-        normed = (normalize(joined[...].astype(F32)) * gain[...]).astype(BF16)
-        raw = jnp.dot(normed, w_head[...], preferred_element_type=F32)
-        confidence = 1.0 + jnp.exp(raw[:, 3 * PIXELS :])
-        for plane in range(4):
-            columns = slice(plane * PIXELS, (plane + 1) * PIXELS)
-            value = confidence if plane == 3 else raw[:, columns] * confidence
-            total[image, :, columns] += value.astype(BF16).astype(F32)
+        raws = []
+        for i in range(HEAD_GROUP):
+            for start, size, ref in zip(STARTS, SIZES, blocks):
+                joined[i, start : start + size] = ref[(step % 2) * HEAD_GROUP + i]
+            raws.append(jnp.dot(joined[i], w_head[...], preferred_element_type=F32))
+        for i in range(HEAD_GROUP):
+            slot = order[step * HEAD_GROUP + i]
+            image = jnp.where(slot < SLOTS, table[slot % SLOTS] % IMG_DEV, IMG_DEV)
+            confidence = 1.0 + jnp.exp(raws[i][:, 3 * PIXELS :])
+            for plane in range(4):
+                columns = slice(plane * PIXELS, (plane + 1) * PIXELS)
+                value = confidence if plane == 3 else raws[i][:, columns] * confidence
+                total[image, :, columns] += value.astype(BF16).astype(F32)
         return carry
 
-    lax.fori_loop(0, count, step, 0)
+    lax.fori_loop(0, steps, one_step, 0)
     for image in range(IMG_DEV):
         out[image * PATCHES : (image + 1) * PATCHES] = total[image, :PATCHES]
 
 
-def head(table, parts, gain, w_head):
+def head(table, parts, w_head):
     any_space = pl.BlockSpec(memory_space=pl.ANY)
     vmem = pl.BlockSpec(memory_space=pltpu.VMEM)
     return pl.pallas_call(
         head_kernel,
         out_shape=jax.ShapeDtypeStruct((IMG_DEV * PATCHES, HEAD_OUT), F32),
-        in_specs=[pl.BlockSpec(memory_space=pltpu.SMEM), *[any_space] * PARTS, vmem, vmem],
+        in_specs=[pl.BlockSpec(memory_space=pltpu.SMEM), *[any_space] * PARTS, vmem],
         out_specs=vmem,
-        scratch_shapes=[pltpu.VMEM((2, size, D_MODEL), BF16) for size in SIZES]
+        scratch_shapes=[pltpu.VMEM((2 * HEAD_GROUP, size, D_MODEL), BF16) for size in SIZES]
         + [
-            pltpu.VMEM((ROWS, D_MODEL), BF16),
-            pltpu.VMEM((IMG_DEV, ROWS, HEAD_OUT), F32),
-            pltpu.SMEM((SLOTS + 1,), jnp.int32),
-            pltpu.SemaphoreType.DMA((PARTS, 2)),
+            pltpu.VMEM((HEAD_GROUP, ROWS, D_MODEL), BF16),
+            pltpu.VMEM((IMG_DEV + 1, ROWS, HEAD_OUT), F32),
+            pltpu.SMEM((SLOTS + HEAD_GROUP,), jnp.int32),
+            pltpu.SemaphoreType.DMA((PARTS, 2 * HEAD_GROUP)),
         ],
         compiler_params=pltpu.CompilerParams(vmem_limit_bytes=60 * 2**20),
         name="head",
-    )(table, *parts, gain, w_head)
+    )(table, *parts, w_head)
 
 
 def per_device(
@@ -530,17 +533,18 @@
 ):
     *parts, table = exchange(
         image_slot,
-        pairs,
+        pairs.T,
         tokens,
         w_embed,
-        gain_query.reshape(1, D_MODEL),
-        gain_key.reshape(1, D_MODEL),
+        gain_query,
+        gain_key,
+        gain_head,
         w_query,
         w_key,
         w_value,
         w_out,
     )
-    return head(table, parts, gain_head.reshape(1, D_MODEL), w_head)
+    return head(table, parts, w_head)
 
 
 def solution(mesh):

time: 204 us -> 161 us (0.79)
  Pallas kernels: 198 us -> 161 us
  local copies, waits for them, and re-layouts: 5.18 us -> 0 us
    pallas_call x1, Pallas kernels: 169 us -> 141 us  [exchange(): pl.pallas_call(exchange_kernel, out_shape=[jax.ShapeDtypeStruct((SLOTS, s...]
    pallas_call x1, Pallas kernels: 28.3 us -> 20.1 us  [head(): pl.pallas_call(head_kernel, out_shape=jax.ShapeDtypeStruct((IMG_DEV * PAT...]
    reshape x3 -> x0, local copies, waits for them, and re-layouts: 3.84 us -> none  [the longest x1 1.28 us: per_device(): gain_key.reshape(1, D_MODEL)]
where the time goes in v2:
time: 161 us
  Pallas kernels  161 us (100%)
    pallas_call x1, Pallas kernels, exchange(): pl.pallas_call(exchange_kernel, out_shape=[jax.ShapeDtypeStruct((SLOTS, s...  141 us
    pallas_call x1, Pallas kernels, head(): pl.pallas_call(head_kernel, out_shape=jax.ShapeDtypeStruct((IMG_DEV * PAT...  20.1 us

profile of v2, /device:TPU:34, one launch (start us, length us, event | category | flops | bytes accessed | tf_op | source)
XLA Modules:
  0.0 161.0 jit_solution(6393649749006024010)
XLA Ops:
  0.0 140.7 %exchange.1 = (bf16[32,48,768]{2,1,0:T(8,128)(2,1)}, bf16[32,48,768]{2,1,0:T(8,128)(2,1)}, bf16[32,48,768]{2,1,0:T(8,128)(2,1)}, bf16[32,52,768]{2,1,0:T(8,128)(2,1)}, s32[32]{0:T(128)}) custom-call(s32[1024]{0:T(1024)} %image_slot.1, s32[2,8]{1,0:T(2,128)} %bitcast.1, bf16[1568,1024]{1,0:T(8,128)(2,1)} %tokens_hbm.1, bf16[1024,768]{1,0:T(8,128)(2,1)} %w_embed_hbm.1, ...), custom_call_target="tpu_custom_call" | custom-call | tf_op jit(solution)/shard_map/exchange/pallas_call | solution.py:398
  140.7 20.1 %head.1 = f32[1568,1024]{1,0:T(8,128)} custom-call(s32[32]{0:T(128)} %get-tuple-element.10.table, bf16[32,48,768]{2,1,0:T(8,128)(2,1)} %get-tuple-element.11.refs_0_, bf16[32,48,768]{2,1,0:T(8,128)(2,1)} %get-tuple-element.12.refs_1_, bf16[32,48,768]{2,1,0:T(8,128)(2,1)} %get-tuple-element.13.refs_2_, bf16[32,52,768]{2,1,0:T(8,128)(2,1)} %get-tuple-element.14.refs_3_, ...), custom_call_target="tpu_custom_call" | custom-call | tf_op jit(solution)/shard_map/head/pallas_call | solution.py:503

commit v3 on v2

--- a/solution.py
+++ b/solution.py
@@ -18,14 +18,16 @@
 N_GX = 8
 N_GY = 16
 SLOTS = 32
-HEAD_GROUP = 4
+COUPLES = IMG_DEV // 2
+DEPTH = 6
 GROUP = 4
-SIZES = (48, 48, 48, 52)
-OUTWARD = (0, 1, 2, 3)
-HOMEWARD = (0, 1, 2, 3)
+SIZES = (16, 48, 48, 48, 36)
+OUTWARD = (1, 2, 3, 4, 0)
+HOMEWARD = (1, 2, 3, 4, 0)
 PARTS = len(SIZES)
 STARTS = tuple(sum(SIZES[:part]) for part in range(PARTS))
 PADDED = tuple(-(-size // 16) * 16 for size in SIZES)
+LAST = HOMEWARD[-1]
 ROWS = STARTS[-1] + PADDED[-1]
 MESH = pl.DeviceIdType.MESH
 BF16 = jnp.bfloat16
@@ -62,9 +64,11 @@
     w_key_hbm,
     w_value_hbm,
     w_out_hbm,
+    w_head_hbm,
     *refs,
 ):
-    back, (table_out,), refs = refs[:PARTS], refs[PARTS : PARTS + 1], refs[PARTS + 1 :]
+    given, table_out, *refs = refs
+    back, refs = list(refs[: PARTS - 1]), refs[PARTS - 1 :]
     send, recv, refs = refs[:PARTS], refs[PARTS : 2 * PARTS], refs[2 * PARTS :]
     (
     tokens,
@@ -73,6 +77,9 @@
     w_key,
     w_value,
     w_out,
+    w_head,
+    last_back,
+    offered,
     embedded,
     views,
     q_all,
@@ -87,6 +94,7 @@
     load_sem,
     list_sem,
     self_sem,
+    head_sem,
     msg_send,
     msg_recv,
     fwd_send,
@@ -96,6 +104,7 @@
     ) = refs
     gx = lax.axis_index("gx")
     gy = lax.axis_index("gy")
+    back.insert(LAST, last_back)
 
     loads = [
         pltpu.make_async_copy(src, dst, load_sem.at[i])
@@ -107,6 +116,7 @@
                 (w_key_hbm, w_key),
                 (w_value_hbm, w_value),
                 (w_out_hbm, w_out),
+                (w_head_hbm, w_head),
             ]
         )
     ]
@@ -307,6 +317,7 @@
         quad = 4 * (D_MODEL // HEADS)
         head_of = lax.broadcasted_iota(jnp.int32, (size, quad), 1) // (D_MODEL // HEADS)
         key_of = lax.broadcasted_iota(jnp.int32, (4 * size, ROWS), 1)
+        at_once = 2 * GROUP if size <= 16 else GROUP
 
         def score(view, features):
             query = q_all[view, place, features]
@@ -338,8 +349,8 @@
 
         def some_views(group, carry):
             items = [
-                (group * GROUP + i, slice(four * quad, (four + 1) * quad))
-                for i in range(GROUP)
+                (group * at_once + i, slice(four * quad, (four + 1) * quad))
+                for i in range(at_once)
                 for four in range(HEADS // 4)
             ]
             weights = [soften(scores) for scores in [score(*item) for item in items]]
@@ -347,7 +358,7 @@
                 gather(*item, weight)
             return carry
 
-        lax.fori_loop(0, 2 * PAIR_DEV // GROUP, some_views, 0)
+        lax.fori_loop(0, 2 * PAIR_DEV // at_once, some_views, 0)
 
         def side(group, carry):
             block = jnp.concatenate(
@@ -380,15 +391,58 @@
 
     for part in HOMEWARD:
         attend(part)
-    for part in range(PARTS):
+    def leave(part):
+        size = PADDED[part]
+        return pltpu.make_async_copy(
+            offered.at[:, pl.ds(0, size)],
+            given.at[:, pl.ds(STARTS[part], size)],
+            head_sem.at[PARTS + part],
+        )
+
+    def contribute(part, landed):
+        size = PADDED[part]
+        exact = slice(STARTS[part], STARTS[part] + SIZES[part])
+        place = slice(STARTS[part], STARTS[part] + size)
+
+        def some_slots(group, carry):
+            for p in range(PAIR_DEV):
+                views[p, exact] = landed[group * PAIR_DEV + p]
+            normed = jnp.concatenate([views[p, place] for p in range(PAIR_DEV)], axis=0)
+            raw = jnp.dot(normed, w_head[...], preferred_element_type=F32)
+            confidence = 1.0 + jnp.exp(raw[:, 3 * PIXELS :])
+            for plane in range(4):
+                columns = slice(plane * PIXELS, (plane + 1) * PIXELS)
+                value = confidence if plane == 3 else raw[:, columns] * confidence
+                value = value.astype(BF16)
+                for p in range(PAIR_DEV):
+                    offered[group * PAIR_DEV + p, :size, columns] = value[p * size : (p + 1) * size]
+            return carry
+
+        lax.fori_loop(0, SLOTS // PAIR_DEV, some_slots, 0)
+
+    previous = None
+    for part in HOMEWARD:
         for copy in self_copies(part):
             copy.wait()
+        wait_copies(part, False, "recv")
+        landed = last_back
+        if part != LAST:
+            landed = recv[part]
+            arrive = pltpu.make_async_copy(back[part], landed, head_sem.at[part])
+            arrive.start()
+            arrive.wait()
+        if previous is not None:
+            previous.wait()
+        contribute(part, landed)
+        previous = leave(part)
+        previous.start()
+    for part in HOMEWARD:
         wait_copies(part, False, "send")
-        wait_copies(part, False, "recv")
+    previous.wait()
 
 
 def exchange(
-    image_slot, pairs, tokens, w_embed, gain_query, gain_key, gain_head, w_query, w_key, w_value, w_out
+    image_slot, pairs, tokens, w_embed, gain_query, gain_key, gain_head, w_query, w_key, w_value, w_out, w_head
 ):
     any_space = pl.BlockSpec(memory_space=pl.ANY)
     smem = pl.BlockSpec(memory_space=pltpu.SMEM)
@@ -397,10 +451,17 @@
     full = pltpu.VMEM((2 * PAIR_DEV, ROWS, D_MODEL), BF16)
     return pl.pallas_call(
         exchange_kernel,
-        out_shape=[jax.ShapeDtypeStruct((SLOTS, size, D_MODEL), BF16) for size in SIZES]
-        + [jax.ShapeDtypeStruct((SLOTS,), jnp.int32)],
-        in_specs=[smem, smem, any_space, any_space, vmem, vmem, vmem] + [any_space] * 4,
-        out_specs=[any_space] * PARTS + [smem],
+        out_shape=[
+            jax.ShapeDtypeStruct((SLOTS, ROWS, HEAD_OUT), BF16),
+            jax.ShapeDtypeStruct((SLOTS,), jnp.int32),
+        ]
+        + [
+            jax.ShapeDtypeStruct((SLOTS, size, D_MODEL), BF16)
+            for part, size in enumerate(SIZES)
+            if part != LAST
+        ],
+        in_specs=[smem, smem, any_space, any_space, vmem, vmem, vmem] + [any_space] * 5,
+        out_specs=[any_space, smem] + [any_space] * (PARTS - 1),
         scratch_shapes=[pltpu.VMEM((SLOTS, size, D_MODEL), BF16) for size in SIZES * 2]
         + [
             pltpu.VMEM((IMG_DEV * PATCHES, D_ENC), BF16),
@@ -409,6 +470,9 @@
             square,
             square,
             square,
+            pltpu.VMEM((D_MODEL, HEAD_OUT), BF16),
+            pltpu.VMEM((SLOTS, SIZES[LAST], D_MODEL), BF16),
+            pltpu.VMEM((SLOTS, max(PADDED), HEAD_OUT), BF16),
             pltpu.VMEM((IMG_DEV, ROWS, D_MODEL), BF16),
             full,
             full,
@@ -420,9 +484,10 @@
             pltpu.SMEM((N_GY + N_GX + 1, 1, 128), jnp.int32),
             pltpu.SMEM((2 * PAIR_DEV,), jnp.int32),
             pltpu.SMEM((SLOTS,), jnp.int32),
-            pltpu.SemaphoreType.DMA((6,)),
+            pltpu.SemaphoreType.DMA((7,)),
             pltpu.SemaphoreType.DMA,
             pltpu.SemaphoreType.DMA((PARTS, 2)),
+            pltpu.SemaphoreType.DMA((2 * PARTS,)),
             pltpu.SemaphoreType.DMA((N_GY + N_GX,)),
             pltpu.SemaphoreType.DMA((N_GY + N_GX,)),
             pltpu.SemaphoreType.DMA((PARTS, N_GY + N_GX)),
@@ -434,87 +499,87 @@
             collective_id=0, has_side_effects=True, vmem_limit_bytes=62 * 2**20
         ),
         name="exchange",
-    )(image_slot, pairs, tokens, w_embed, gain_query, gain_key, gain_head, w_query, w_key, w_value, w_out)
-
-
-def head_kernel(table, *refs):
-    sources, (w_head, out), refs = refs[:PARTS], refs[PARTS : PARTS + 2], refs[PARTS + 2 :]
-    blocks, (joined, total, order, sems) = refs[:PARTS], refs[PARTS:]
-
-    def collect(slot, count):
-        order[count] = slot
-        return count + jnp.where(table[slot] >= IMG_DEV, 1, 0)
-
-    count = lax.fori_loop(0, SLOTS, collect, jnp.int32(0))
-
-    for i in range(HEAD_GROUP - 1):
-        order[count + i] = SLOTS
-    steps = (count + HEAD_GROUP - 1) // HEAD_GROUP
-
-    def copies(step):
-        for i in range(HEAD_GROUP):
-            slot = order[step * HEAD_GROUP + i] % SLOTS
-            place = (step % 2) * HEAD_GROUP + i
-            for part in range(PARTS):
-                yield pltpu.make_async_copy(
-                    sources[part].at[slot], blocks[part].at[place], sems.at[part, place]
-                )
-
-    @pl.when(steps > 0)
-    def _():
-        for copy in copies(0):
-            copy.start()
-
+    )(image_slot, pairs, tokens, w_embed, gain_query, gain_key, gain_head, w_query, w_key, w_value, w_out, w_head)
+
+
+def sum_kernel(table, source, out, block, total, staged, first, order, sems, out_sems):
+    def place_of(slot):
+        return jnp.where(table[slot] >= IMG_DEV, (table[slot] % IMG_DEV) // 2, COUPLES)
+
+    for couple in range(COUPLES + 1):
+        first[couple] = 0
+
+    def tally(slot, carry):
+        couple = place_of(slot)
+        first[couple] = first[couple] + 1
+        return carry
+
+    lax.fori_loop(0, SLOTS, tally, 0)
+    bounds = [jnp.int32(0)]
+    for couple in range(COUPLES):
+        bounds.append(bounds[-1] + first[couple])
+    for couple in range(COUPLES + 1):
+        first[couple] = bounds[couple]
+
+    def arrange(slot, carry):
+        couple = place_of(slot)
+        order[first[couple]] = slot
+        first[couple] = first[couple] + 1
+        return carry
+
+    lax.fori_loop(0, SLOTS, arrange, 0)
+    count = bounds[-1]
+
+    def copy(item):
+        place = item % DEPTH
+        return pltpu.make_async_copy(source.at[order[item]], block.at[place], sems.at[place])
+
+    def start(item):
+        @pl.when(item < count)
+        def _():
+            copy(item).start()
+
+    for item in range(DEPTH - 1):
+        start(item)
     total[...] = jnp.zeros_like(total)
-    for i in range(HEAD_GROUP):
-        joined[i, STARTS[-1] :] = jnp.zeros((PADDED[-1], D_MODEL), BF16)
-
-    def one_step(step, carry):
-        @pl.when(step + 1 < steps)
-        def _():
-            for copy in copies(step + 1):
-                copy.start()
-
-        for copy in copies(step):
-            copy.wait()
-        raws = []
-        for i in range(HEAD_GROUP):
-            for start, size, ref in zip(STARTS, SIZES, blocks):
-                joined[i, start : start + size] = ref[(step % 2) * HEAD_GROUP + i]
-            raws.append(jnp.dot(joined[i], w_head[...], preferred_element_type=F32))
-        for i in range(HEAD_GROUP):
-            slot = order[step * HEAD_GROUP + i]
-            image = jnp.where(slot < SLOTS, table[slot % SLOTS] % IMG_DEV, IMG_DEV)
-            confidence = 1.0 + jnp.exp(raws[i][:, 3 * PIXELS :])
-            for plane in range(4):
-                columns = slice(plane * PIXELS, (plane + 1) * PIXELS)
-                value = confidence if plane == 3 else raws[i][:, columns] * confidence
-                total[image, :, columns] += value.astype(BF16).astype(F32)
+
+    def one_item(item, carry):
+        start(item + DEPTH - 1)
+        copy(item).wait()
+        total[table[order[item]] % IMG_DEV] += block[item % DEPTH].astype(F32)
         return carry
 
-    lax.fori_loop(0, steps, one_step, 0)
-    for image in range(IMG_DEV):
-        out[image * PATCHES : (image + 1) * PATCHES] = total[image, :PATCHES]
-
-
-def head(table, parts, w_head):
+    leaving = []
+    for couple in range(COUPLES):
+        lax.fori_loop(bounds[couple], bounds[couple + 1], one_item, 0)
+        for image in (2 * couple, 2 * couple + 1):
+            staged[image * PATCHES : (image + 1) * PATCHES] = total[image, :PATCHES]
+        rows = slice(2 * couple * PATCHES, 2 * (couple + 1) * PATCHES)
+        leaving.append(pltpu.make_async_copy(staged.at[rows], out.at[rows], out_sems.at[couple]))
+        leaving[-1].start()
+    for parting in leaving:
+        parting.wait()
+
+
+def sum_slots(table, contributions):
     any_space = pl.BlockSpec(memory_space=pl.ANY)
-    vmem = pl.BlockSpec(memory_space=pltpu.VMEM)
     return pl.pallas_call(
-        head_kernel,
+        sum_kernel,
         out_shape=jax.ShapeDtypeStruct((IMG_DEV * PATCHES, HEAD_OUT), F32),
-        in_specs=[pl.BlockSpec(memory_space=pltpu.SMEM), *[any_space] * PARTS, vmem],
-        out_specs=vmem,
-        scratch_shapes=[pltpu.VMEM((2 * HEAD_GROUP, size, D_MODEL), BF16) for size in SIZES]
-        + [
-            pltpu.VMEM((HEAD_GROUP, ROWS, D_MODEL), BF16),
-            pltpu.VMEM((IMG_DEV + 1, ROWS, HEAD_OUT), F32),
-            pltpu.SMEM((SLOTS + HEAD_GROUP,), jnp.int32),
-            pltpu.SemaphoreType.DMA((PARTS, 2 * HEAD_GROUP)),
+        in_specs=[pl.BlockSpec(memory_space=pltpu.SMEM), any_space],
+        out_specs=any_space,
+        scratch_shapes=[
+            pltpu.VMEM((DEPTH, ROWS, HEAD_OUT), BF16),
+            pltpu.VMEM((IMG_DEV, ROWS, HEAD_OUT), F32),
+            pltpu.VMEM((IMG_DEV * PATCHES, HEAD_OUT), F32),
+            pltpu.SMEM((COUPLES + 1,), jnp.int32),
+            pltpu.SMEM((SLOTS,), jnp.int32),
+            pltpu.SemaphoreType.DMA((DEPTH,)),
+            pltpu.SemaphoreType.DMA((COUPLES,)),
         ],
         compiler_params=pltpu.CompilerParams(vmem_limit_bytes=60 * 2**20),
-        name="head",
-    )(table, *parts, w_head)
+        name="sum_slots",
+    )(table, contributions)
 
 
 def per_device(
@@ -531,7 +596,7 @@
     gain_head,
     w_head,
 ):
-    *parts, table = exchange(
+    contributions, table, *_ = exchange(
         image_slot,
         pairs.T,
         tokens,
@@ -543,8 +608,9 @@
         w_key,
         w_value,
         w_out,
+        w_head,
     )
-    return head(table, parts, w_head)
+    return sum_slots(table, contributions)
 
 
 def solution(mesh):

time: 161 us -> 158 us (0.981)
  the two profiles are of different devices: /device:TPU:34 before, /device:TPU:68 now
where the time goes in v3:
time: 158 us; the launch traced here: 157 us
  Pallas kernels  157 us (99%)
    pallas_call x1, Pallas kernels, exchange(): pl.pallas_call(exchange_kernel, out_shape=[jax.ShapeDtypeStruct((SLOTS, R...  148 us
    pallas_call x1, Pallas kernels, sum_slots(): pl.pallas_call(sum_kernel, out_shape=jax.ShapeDtypeStruct((IMG_DEV * PATC...  9.22 us

profile of v3, /device:TPU:68, one launch (start us, length us, event | category | flops | bytes accessed | tf_op | source)
XLA Modules:
  0.0 157.5 jit_solution(18204600157059720827)
XLA Ops:
  0.0 148.1 %exchange.1 = (bf16[32,208,1024]{2,1,0:T(8,128)(2,1)}, s32[32]{0:T(128)}, bf16[32,48,768]{2,1,0:T(8,128)(2,1)}, bf16[32,48,768]{2,1,0:T(8,128)(2,1)}, bf16[32,48...) custom-call(s32[1024]{0:T(1024)} %image_slot.1, s32[2,8]{1,0:T(2,128)} %bitcast.1, bf16[1568,1024]{1,0:T(8,128)(2,1)} %tokens_hbm.1, ...), custom_call_target="tpu_custom_call" | custom-call | tf_op jit(solution)/shard_map/exchange/pallas_call | solution.py:452
  148.1 9.2 %sum_slots.1 = f32[1568,1024]{1,0:T(8,128)} custom-call(s32[32]{0:T(128)} %get-tuple-element.7.table, bf16[32,208,1024]{2,1,0:T(8,128)(2,1)} %get-tuple-element.8.source), custom_call_target="tpu_custom_call" | custom-call | tf_op jit(solution)/shard_map/sum_slots/pallas_call | solution.py:566

commit v4 on v3

--- a/solution.py
+++ b/solution.py
@@ -307,8 +307,6 @@
 
     for part in OUTWARD:
         project(part)
-    for part in range(PARTS):
-        wait_copies(part, True, "send")
 
     def attend(part):
         size = PADDED[part]
@@ -373,6 +371,8 @@
             return carry
 
         lax.fori_loop(0, 2, side, 0)
+
+        wait_copies(part, True, "send")
 
         def pack(slot, carry):
             send[part][slot] = views[lists[N_GY + N_GX, 0, slot], exact]

time: 158 us -> 157 us (level)
  the two profiles are of different devices: /device:TPU:68 before, /device:TPU:102 now
where the time goes in v4:
time: 157 us
  Pallas kernels  157 us (100%)
    pallas_call x1, Pallas kernels, exchange(): pl.pallas_call(exchange_kernel, out_shape=[jax.ShapeDtypeStruct((SLOTS, R...  148 us
    pallas_call x1, Pallas kernels, sum_slots(): pl.pallas_call(sum_kernel, out_shape=jax.ShapeDtypeStruct((IMG_DEV * PATC...  8.55 us

profile of v4, /device:TPU:102, one launch (start us, length us, event | category | flops | bytes accessed | tf_op | source)
XLA Modules:
  0.0 156.7 jit_solution(8220973372965157586)
XLA Ops:
  0.0 148.0 %exchange.1 = (bf16[32,208,1024]{2,1,0:T(8,128)(2,1)}, s32[32]{0:T(128)}, bf16[32,48,768]{2,1,0:T(8,128)(2,1)}, bf16[32,48,768]{2,1,0:T(8,128)(2,1)}, bf16[32,48...) custom-call(s32[1024]{0:T(1024)} %image_slot.1, s32[2,8]{1,0:T(2,128)} %bitcast.1, bf16[1568,1024]{1,0:T(8,128)(2,1)} %tokens_hbm.1, ...), custom_call_target="tpu_custom_call" | custom-call | tf_op jit(solution)/shard_map/exchange/pallas_call | solution.py:452
  148.0 8.5 %sum_slots.1 = f32[1568,1024]{1,0:T(8,128)} custom-call(s32[32]{0:T(128)} %get-tuple-element.7.table, bf16[32,208,1024]{2,1,0:T(8,128)(2,1)} %get-tuple-element.8.source), custom_call_target="tpu_custom_call" | custom-call | tf_op jit(solution)/shard_map/sum_slots/pallas_call | solution.py:566
